TPU v7x, 32 devices: a whole 2x2x4 slice. The times are simulated.
32 devices in a mesh: rep: 4 (over y, core), ep: 8 (over z, x).
Axes of the slice: x: 2, y: 2, z: 4, core: 2. Of those that a mesh axis runs over, the one named last changes fastest.
Arguments:
- tokens: bfloat16 [4096, 2048], P(('rep', 'ep')), may hold values from -6 to 6
- norm_gain: float32 [2048], replicated, may hold values from 0.5 to 1.5
- gates: float32 [4096], P(('rep', 'ep')), may hold values from 0.25 to 1
- expert_ids: int32 [4096], P(('rep', 'ep')), may hold values from 0 to 7, as said below
- slots: int32 [4096], P(('rep', 'ep')), may hold values from 0 to 15, as said below
- dropped: int32 [4096], P(('rep', 'ep')), may hold values from 0 to 1
- res_in: bfloat16 [2048, 4096], P('ep', 'rep'), may hold values from -0.125 to 0.125
- res_out: bfloat16 [4096, 2048], P('rep', 'ep'), may hold values from -0.09375 to 0.09375
- expert_in: bfloat16 [8, 2048, 4096], P('ep', None, 'rep'), may hold values from -0.125 to 0.125
- expert_out: bfloat16 [8, 4096, 2048], P('ep', 'rep'), may hold values from -0.09375 to 0.09375
Outputs:
- mixed: bfloat16 [4096, 2048], P(('rep', 'ep'))
Inputs may be any that keep to these rules, and one draw needn't show every extreme that they name: `expert_ids`: within the tokens of one device, two tokens with the same expert and dropped = 0 have different slots; slots count such tokens in order, and a token is dropped exactly when 16 earlier tokens of its device chose its expert. In every draw some expert receives at least 2 tokens from every device. `slots`: slot of a dropped token is 0.
All inputs are finite; a program needn't handle non-finite values.
Results may differ from a plain program's by a relative error of at most 0.0045.
Values may be sent and summed in bfloat16 or wider, within the bound.
A program may use at most 128 MiB of HBM per device.

v0:
```python
import jax
import jax.numpy as jnp
from jax import lax
from jax.sharding import PartitionSpec as P


def rms_norm(tokens, norm_gain):
    values = tokens.astype(jnp.float32)
    scale = lax.rsqrt(jnp.mean(values * values, axis=-1, keepdims=True) + 1e-06)
    return (values * scale * norm_gain).astype(jnp.bfloat16)


def on_device(
    tokens, norm_gain, gates, expert_ids, slots, dropped, res_in, res_out, expert_in, expert_out
):
    n_rep = lax.axis_size("rep")
    n_ep = lax.axis_size("ep")
    rows = tokens.shape[0]
    width = tokens.shape[1]
    cap = rows // n_ep
    normed = rms_norm(tokens, norm_gain)
    keep = 1 - dropped
    gathered, ids_all, slots_all, keep_all = (
        lax.all_gather(normed, "rep", axis=0, tiled=True),
        lax.all_gather(expert_ids, "rep", axis=0, tiled=True),
        lax.all_gather(slots, "rep", axis=0, tiled=True),
        lax.all_gather(keep, "rep", axis=0, tiled=True),
    )
    replica = jnp.arange(n_rep * rows, dtype=jnp.int32) // rows
    target = ids_all * (n_rep * cap) + replica * cap + slots_all
    places = jnp.arange(n_ep * n_rep * cap, dtype=jnp.int32)
    table = ((target[None, :] == places[:, None]) & (keep_all[None, :] == 1)).astype(jnp.bfloat16)
    buffer = (
        jnp.dot(table, gathered, preferred_element_type=jnp.float32)
        .astype(jnp.bfloat16)
        .reshape(n_ep, n_rep * cap, width)
    )
    block = lax.all_to_all(buffer, "ep", split_axis=0, concat_axis=0, tiled=True)
    flat = block.reshape(-1, width)
    hidden = jax.nn.gelu(
        jnp.dot(flat, expert_in[0], preferred_element_type=jnp.float32), approximate=True
    ).astype(jnp.bfloat16)
    result = jnp.dot(hidden, expert_out[0], preferred_element_type=jnp.float32)
    back = lax.all_to_all(
        result.reshape(block.shape[0], block.shape[1], width).astype(jnp.bfloat16),
        "ep",
        split_axis=0,
        concat_axis=0,
        tiled=True,
    ).astype(jnp.float32)
    picked = jnp.take(back.reshape(-1, width), jnp.where(keep_all == 1, target, 0), axis=0)
    partial_rows = jnp.where(keep_all[:, None] == 1, picked, 0.0)
    weight_in = lax.all_gather(res_in, "ep", axis=0, tiled=True)
    hidden = jax.nn.gelu(
        jnp.dot(gathered, weight_in, preferred_element_type=jnp.float32), approximate=True
    ).astype(jnp.bfloat16)
    weight_out = lax.all_gather(res_out, "ep", axis=1, tiled=True)
    res_branch = lax.psum_scatter(
        jnp.dot(hidden, weight_out, preferred_element_type=jnp.float32),
        "rep",
        scatter_dimension=0,
        tiled=True,
    )
    exp_branch = lax.psum_scatter(partial_rows, "rep", scatter_dimension=0, tiled=True)
    mixed = tokens.astype(jnp.float32) + res_branch + gates[:, None] * exp_branch
    return mixed.astype(jnp.bfloat16)


def solution(mesh):
    return jax.shard_map(
        on_device,
        mesh=mesh,
        in_specs=(
            P(("rep", "ep"), None),
            P(),
            P(("rep", "ep")),
            P(("rep", "ep")),
            P(("rep", "ep")),
            P(("rep", "ep")),
            P("ep", "rep"),
            P("rep", "ep"),
            P("ep", None, "rep"),
            P("ep", "rep", None),
        ),
        out_specs=P(("rep", "ep"), None),
        check_vma=False,
    )
```

profile of v0, /device:TPU:0, one launch (start us, length us, event | category | flops | bytes accessed | tf_op | source)
XLA Modules:
  0.0 360.6 jit_solution(16574335060905642381)
XLA Ops:
  6.5 0.0 copy-start.5
  6.5 0.0 copy-start.1
  6.5 0.0 copy-start.2
  6.5 0.0 all-gather.7.cloned.1.call-start
  6.5 1.3 fusion.25
  7.8 2.0 fusion.27
  9.8 0.0 all-gather.7.cloned.1.call-update
  9.9 0.0 all-gather.11.cloned.1.call-start
  9.9 0.7 all-gather.11.cloned.1.call-update
  10.6 0.0 all-gather.9.cloned.1.call-start
  10.7 0.7 all-gather.9.cloned.1.call-update
  11.4 0.0 copy-done.5
  11.4 6.0 %all-gather = s32[4,1,128]{2,1,0:T(1,128)S(1)} all-gather(s32[1,1,128]{2,1,0:T(1,128)S(1)} %subtract_bitcast_fusion), channel_id=1, replica_groups=mesh['rep'=4,'ep'=8] {'rep'}, dimensions={0}, use_global_device_ids=true | all-gather | bytes 2560 | tf_op jit(solution)/shard_map/all_gather | solution.py:27
  17.4 0.0 copy-done.1
  17.4 5.3 %all-gather.2 = s32[4,1,128]{2,1,0:T(1,128)S(1)} all-gather(s32[1,1,128]{2,1,0:T(1,128)S(1)} %bitcast.38), channel_id=1, replica_groups=mesh['rep'=4,'ep'=8] {'rep'}, dimensions={0}, use_global_device_ids=true | all-gather | bytes 2560 | tf_op jit(solution)/shard_map/all_gather | solution.py:26
  22.7 0.0 copy-done.2
  22.7 5.0 %all-gather.1 = s32[4,1,128]{2,1,0:T(1,128)S(1)} all-gather(s32[1,1,128]{2,1,0:T(1,128)S(1)} %bitcast.39), channel_id=1, replica_groups=mesh['rep'=4,'ep'=8] {'rep'}, dimensions={0}, use_global_device_ids=true | all-gather | bytes 2560 | tf_op jit(solution)/shard_map/all_gather | solution.py:25
  27.8 7.6 %all-gather.7.cloned.1.call-done = bf16[512,2048]{1,0:T(8,128)(2,1)} async-done(((bf16[128,2048]{1,0:T(8,128)(2,1)}), bf16[512,2048]{1,0:T(8,128)(2,1)}) %all-gather.7.cloned.1.call-update) | async-done | bytes 2097168 | tf_op jit(solution)/shard_map/all_gather | solution.py:24
  35.3 4.2 %convolution_convert_fusion = bf16[512,2048]{1,0:T(8,128)(2,1)} fusion(bf16[512,2048]{1,0:T(8,128)(2,1)} %all-gather.7.cloned.1.call-done, s32[512]{0:T(512)S(1)} %get-tuple-element.7, pred[512]{0:T(512)(128)(4,1)S(1)} %bitcast.36), kind=kOutput, calls=%fused_computation.9 | convolution fusion | flops 1075314688 | bytes 4196864 | tf_op jit(solution)/shard_map/dot_general | solution.py:34
  39.5 5.5 %all-to-all-start = ((bf16[8,64,2048]{2,1,0:T(8,128)(2,1)}), bf16[8,64,2048]{2,1,0:T(8,128)(2,1)S(1)}, u32[]{:S(2)}, u32[]{:S(2)}) async-start(bf16[8,64,2048]{2,1,0:T(8,128)(2,1)} %bitcast.33), calls=%async_computation.1 | async-start | bytes 4194304 | tf_op jit(solution)/shard_map/all_to_all | solution.py:38
  45.0 0.0 reduce-scatter.3.cloned.1.call-start
  45.1 102.0 %all-gather.11.cloned.1.call-done = bf16[1024,2048]{1,0:T(8,128)(2,1)} async-done(((bf16[1024,256]{1,0:T(8,128)(2,1)}), bf16[1024,2048]{1,0:T(8,128)(2,1)}) %all-gather.11.cloned.1.call-update) | async-done | bytes 4194320 | tf_op jit(solution)/shard_map/all_gather | solution.py:57
  147.1 74.9 %all-gather.9.cloned.1.call-done = bf16[2048,1024]{1,0:T(8,128)(2,1)} async-done(((bf16[256,1024]{1,0:T(8,128)(2,1)}), bf16[2048,1024]{1,0:T(8,128)(2,1)}) %all-gather.9.cloned.1.call-update) | async-done | bytes 4194320 | tf_op jit(solution)/shard_map/all_gather | solution.py:53
  221.9 10.9 %fusion.30 = f32[512,2048]{1,0:T(8,128)} fusion(bf16[1024,2048]{1,0:T(8,128)(2,1)} %all-gather.11.cloned.1.call-done, bf16[512,2048]{1,0:T(8,128)(2,1)} %all-gather.7.cloned.1.call-done, bf16[2048,1024]{1,0:T(8,128)(2,1)} %all-gather.9.cloned.1.call-done), kind=kOutput, calls=%fused_computation.35 | convolution fusion | flops 4299685888 | bytes 14680064 | tf_op jit(solution)/shard_map/dot_general | solution.py:59
  232.8 0.0 reduce-scatter.3.cloned.1.call-update
  232.9 0.0 all-to-all-done
  232.9 0.0 copy-start.4
  232.9 5.1 %fusion.22 = bf16[512,1024]{1,0:T(8,128)(2,1)S(1)} fusion(bf16[512,2048]{1,0:T(8,128)(2,1)S(1)} %bitcast.32, bf16[1,2048,1024]{2,1,0:T(8,128)(2,1)} %param.18), kind=kOutput, calls=%fused_computation.25 | convolution fusion | flops 2152202240 | bytes 7340032 | tf_op jit(solution)/shard_map/dot_general | solution.py:41
  237.9 0.0 copy-done.4
  238.0 3.7 %fusion.4 = bf16[8,64,2048]{2,1,0:T(8,128)(2,1)} fusion(bf16[8,64,1024]{2,1,0:T(8,128)(2,1)S(1)} %bitcast.40, bf16[1,1024,2048]{2,1,0:T(8,128)(2,1)S(1)} %copy-done.4), kind=kOutput, calls=%fused_computation.8 | convolution fusion | flops 2148532224 | bytes 7340032 | tf_op jit(solution)/shard_map/dot_general | solution.py:43
  241.7 3.6 all-to-all-start.1
  245.3 0.2 reduce-scatter.5.cloned.1.call-start
  245.5 47.4 %all-to-all-done.1 = bf16[8,64,2048]{2,1,0:T(8,128)(2,1)S(1)} async-done(((bf16[8,64,2048]{2,1,0:T(8,128)(2,1)}), bf16[8,64,2048]{2,1,0:T(8,128)(2,1)S(1)}, u32[]{:S(2)}, u32[]{:S(2)}) %all-to-all-start.1) | async-done | bytes 2097184 | tf_op jit(solution)/shard_map/all_to_all | solution.py:44
  292.9 2.6 bitcast_convert_fusion
  295.6 7.6 %gather_fusion = f32[512,2048]{1,0:T(8,128)} fusion(f32[512,2048]{1,0:T(8,128)} %bitcast_convert_fusion, s32[1024]{0:T(1024)S(1)} %pad_clamp_fusion), kind=kCustom, calls=%fused_computation | custom fusion | bytes 8390656 | tf_op jit(solution)/shard_map/jit(_take)/gather | solution.py:51
  303.2 4.6 %select_select_fusion = f32[512,2048]{1,0:T(8,128)} fusion(f32[512,2048]{1,0:T(8,128)} %gather_fusion, pred[512]{0:T(512)(128)(4,1)S(1)} %get-tuple-element.5, pred[512]{0:T(512)(128)(4,1)S(1)} %bitcast.37), kind=kLoop, calls=%fused_computation.5 | loop fusion | flops 2097152 | bytes 8389632 | tf_op jit(solution)/shard_map/jit(_where)/select_n | solution.py:52
  307.8 0.0 copy-start
  307.8 0.0 copy-start.3
  307.8 0.0 reduce-scatter.5.cloned.1.call-update
  307.8 0.0 reduce-scatter.3.cloned.1.call-done
  307.8 43.7 %reduce-scatter.5.cloned.1.call-done = f32[128,2048]{1,0:T(8,128)} async-done(((f32[512,2048]{1,0:T(8,128)}), f32[128,2048]{1,0:T(8,128)}) %reduce-scatter.5.cloned.1.call-update) | async-done | bytes 1048592 | tf_op jit(solution)/shard_map/reduce_scatter | solution.py:64
  351.5 0.0 copy-done
  351.5 0.0 copy-done.3
  351.5 2.5 fusion.29
  (6 shorter events, 0.1 us)
Async XLA Ops:
  6.5 4.8 %copy-start.5 = (s32[128]{0:T(128)S(1)}, s32[128]{0:T(128)}, u32[]{:S(2)}) copy-start(s32[128]{0:T(128)} %param.15) | copy-start | bytes 1540
  6.5 10.8 %copy-start.1 = (s32[128]{0:T(128)S(1)}, s32[128]{0:T(128)}, u32[]{:S(2)}) copy-start(s32[128]{0:T(128)} %param.14) | copy-start | bytes 1540
  6.5 16.1 %copy-start.2 = (s32[128]{0:T(128)S(1)}, s32[128]{0:T(128)}, u32[]{:S(2)}) copy-start(s32[128]{0:T(128)} %param.13) | copy-start | bytes 1540
  6.5 28.8 %all-gather.7.cloned.1.call-start = ((), (), s32[]{:S(2)}) async-start(), calls=%async_computation.4 | async-start | bytes 2621440 | tf_op jit(solution)/shard_map/all_gather | solution.py:24
  9.9 137.2 %all-gather.11.cloned.1.call-start = ((), (), s32[]{:S(2)}) async-start(), calls=%async_computation.6 | async-start | bytes 4718592 | tf_op jit(solution)/shard_map/all_gather | solution.py:57
  10.6 211.3 %all-gather.9.cloned.1.call-start = ((), (), s32[]{:S(2)}) async-start(), calls=%async_computation.5 | async-start | bytes 4718592 | tf_op jit(solution)/shard_map/all_gather | solution.py:53
  39.5 193.4 %all-to-all-start = ((bf16[8,64,2048]{2,1,0:T(8,128)(2,1)}), bf16[8,64,2048]{2,1,0:T(8,128)(2,1)S(1)}, u32[]{:S(2)}, u32[]{:S(2)}) async-start(bf16[8,64,2048]{2,1,0:T(8,128)(2,1)} %bitcast.33), calls=%async_computation.1 | async-start | bytes 4194304 | tf_op jit(solution)/shard_map/all_to_all | solution.py:38
  45.0 262.8 %reduce-scatter.3.cloned.1.call-start = ((), (), s32[]{:S(2)}) async-start(), calls=%async_computation.7 | async-start | bytes 5242880 | tf_op jit(solution)/shard_map/reduce_scatter | solution.py:58
  232.9 5.1 %copy-start.4 = (bf16[1,1024,2048]{2,1,0:T(8,128)(2,1)S(1)}, bf16[1,1024,2048]{2,1,0:T(8,128)(2,1)}, u32[]{:S(2)}) copy-start(bf16[1,1024,2048]{2,1,0:T(8,128)(2,1)} %param.19) | copy-start | bytes 12582916
  241.7 51.3 %all-to-all-start.1 = ((bf16[8,64,2048]{2,1,0:T(8,128)(2,1)}), bf16[8,64,2048]{2,1,0:T(8,128)(2,1)S(1)}, u32[]{:S(2)}, u32[]{:S(2)}) async-start(bf16[8,64,2048]{2,1,0:T(8,128)(2,1)} %fusion.4), calls=%async_computation.2 | async-start | bytes 4194304 | tf_op jit(solution)/shard_map/all_to_all | solution.py:44
  245.3 106.2 %reduce-scatter.5.cloned.1.call-start = ((), (), s32[]{:S(2)}) async-start(), calls=%async_computation.8 | async-start | bytes 5242880 | tf_op jit(solution)/shard_map/reduce_scatter | solution.py:64
  307.8 43.7 %copy-start = (bf16[128,2048]{1,0:T(8,128)(2,1)S(1)}, bf16[128,2048]{1,0:T(8,128)(2,1)}, u32[]{:S(2)}) copy-start(bf16[128,2048]{1,0:T(8,128)(2,1)} %param.10) | copy-start | bytes 1572868
  307.8 43.7 %copy-start.3 = (f32[128]{0:T(128)S(1)}, f32[128]{0:T(128)}, u32[]{:S(2)}) copy-start(f32[128]{0:T(128)} %param.12) | copy-start | bytes 1540
Sparse Core Ops, SparseCore 0:
  10.0 25.2 all-gather.6
  37.4 109.6 all-gather.10
  149.2 72.6 all-gather.8
  233.0 42.7 reduce-scatter.2
  307.9 43.5 reduce-scatter.4
where the time goes:
time: 361 us
  waiting for transfers between devices  277 us (77%)
  matrix products  23.8 us (7%)
  blocking collectives  16.3 us (5%)
  between operations  13.2 us (4%)
  other arithmetic  13.1 us (4%)
  starting transfers between devices  9.45 us (3%)
  local copies, waits for them, and re-layouts  7.62 us (2%)
    all_gather x1, waiting for transfers between devices, on_device(): weight_out = lax.all_gather(res_out, 'ep', axis=1, tiled=True)  102 us
    all_gather x1, waiting for transfers between devices, on_device(): weight_in = lax.all_gather(res_in, 'ep', axis=0, tiled=True)  74.9 us
    all_to_all x1, waiting for transfers between devices, on_device(): lax.all_to_all(result.reshape(block.shape[0], block.shape[1], width).asty...  47.4 us
    reduce_scatter x1, waiting for transfers between devices, on_device(): lax.psum_scatter(partial_rows, 'rep', scatter_dimension=0, tiled=True)  43.7 us
    dot_general x1, matrix products, on_device(): jnp.dot(hidden, weight_out, preferred_element_type=jnp.float32)  10.9 us
    gather x1, local copies, waits for them, and re-layouts, on_device(): jnp.take(back.reshape(-1, width), jnp.where(keep_all == 1, target, 0), ax...  7.6 us
    all_gather x1, waiting for transfers between devices, on_device(): lax.all_gather(normed, 'rep', axis=0, tiled=True)  7.58 us
  transfers between devices with their start and end apart: 7, of which 5 were waited for; matrix products, arithmetic and copies ran while one was open for 11% of the time, Pallas kernels for 0%

commit v1 on v0

--- a/solution.py
+++ b/solution.py
@@ -1,7 +1,371 @@
 import jax
 import jax.numpy as jnp
 from jax import lax
+from jax.experimental import pallas as pl
+from jax.experimental.pallas import tpu as pltpu
 from jax.sharding import PartitionSpec as P
+
+F32 = jnp.float32
+BF16 = jnp.bfloat16
+PLANES = 4
+
+
+def gelu(x):
+    return x * (0.5 * (1.0 + jnp.tanh(0.7978845608028654 * (x + 0.044715 * (x * x * x)))))
+
+
+def dot(a, b):
+    return jnp.dot(a, b, preferred_element_type=F32)
+
+
+def layer_kernel(
+    tokens, gain, gates, ids, slots, dropped, res_in, res_out, exp_in, exp_out,
+    out,
+    w1, w2, ein, eout, normed, xrows, disp, ehid,
+    er_send, er_keep, er_recv, ey_send, ey_keep, ey_recv, eb_send, back,
+    rhid, pc_send, pc_keep, pc_recv, px_send, px_keep, px_recv, py_send, py_keep, py_recv,
+    res,
+    local_sem, wx_ssem, wx_rsem, w1_ssem, w1_rsem, w2_ssem, w2_rsem,
+    n_ssem, n_rsem, d_ssem, d_rsem, x_ssem, x_rsem, e_ssem, e_rsem, b_ssem, b_rsem,
+    r_ssem, r_rsem,
+):
+    rep, ep = lax.axis_index("rep"), lax.axis_index("ep")
+    y, c = rep // 2, rep % 2
+    z, x = ep // 2, ep % 2
+    rows, width = tokens.shape
+    n_ep = 2 * PLANES
+    cap = rows // n_ep
+    half = w1.shape[1]
+    chunk = res_in.shape[0]
+    cols = 2 * chunk
+
+    def dev(r, e):
+        return {"rep": r, "ep": e}
+
+    core_dev = dev(rep + 1 - 2 * c, ep)
+    y_dev = dev(rep + 2 - 4 * y, ep)
+    x_dev = dev(rep, ep + 1 - 2 * x)
+    up_dev, down_dev = dev(rep, ep + 2), dev(rep, ep - 2)
+
+    def peer(k):
+        return lax.rem(ep + k, n_ep)
+
+    def remote(src, dst, ssem, rsem, device):
+        return pltpu.make_async_remote_copy(
+            src_ref=src, dst_ref=dst, send_sem=ssem, recv_sem=rsem,
+            device_id=device, device_id_type=pl.DeviceIdType.MESH,
+        )
+
+    def arrived(dst, ssem, rsem):
+        remote(dst, dst, ssem, rsem, core_dev).wait_recv()
+
+    sent = []
+
+    def send(src, dst, ssem, rsem, device):
+        copy = remote(src, dst, ssem, rsem, device)
+        copy.start()
+        sent.append(copy)
+
+    def at(i, n):
+        return pl.ds(pl.multiple_of(i * n, n), n)
+
+    barrier = pltpu.get_barrier_semaphore()
+    for k in range(1, n_ep):
+        pl.semaphore_signal(
+            barrier, inc=1, device_id=dev(rep, peer(k)), device_id_type=pl.DeviceIdType.MESH
+        )
+    for device in (core_dev, y_dev):
+        pl.semaphore_signal(barrier, inc=1, device_id=device, device_id_type=pl.DeviceIdType.MESH)
+
+    own_w1 = pltpu.make_async_copy(res_in.at[:, at(x, half)], w1.at[at(ep, chunk), :], local_sem.at[0])
+    own_w2 = pltpu.make_async_copy(
+        res_out.at[at(x, half), :], w2.at[z, :, at(x, chunk)], local_sem.at[1]
+    )
+    load_in = pltpu.make_async_copy(exp_in, ein, local_sem.at[2])
+    load_out = pltpu.make_async_copy(exp_out, eout, local_sem.at[3])
+    for copy in (own_w1, own_w2, load_in, load_out):
+        copy.start()
+
+    pl.semaphore_wait(barrier, n_ep + 1)
+
+    send(res_in.at[:, at(1 - x, half)], w1.at[at(ep, chunk), :], wx_ssem.at[0], wx_rsem.at[0], x_dev)
+    send(
+        res_out.at[at(1 - x, half), :], w2.at[z, :, at(x, chunk)],
+        wx_ssem.at[1], wx_rsem.at[1], x_dev,
+    )
+
+    values = tokens[...].astype(F32)
+    scale = lax.rsqrt(jnp.mean(values * values, axis=-1, keepdims=True) + 1e-06)
+    own_normed = (values * scale * gain[...]).astype(BF16)
+
+    def n_at(cc, xx, yy):
+        return normed.at[at(cc * 4 + xx * 2 + yy, rows), :]
+
+    normed[at(c * 4 + x * 2 + y, rows), :] = own_normed
+
+    target = ids[...] * cap + slots[...]
+    places = lax.broadcasted_iota(jnp.int32, (n_ep * cap, rows), 0)
+    table = jnp.where((places == target) & (dropped[...] == 0), 1.0, 0.0).astype(BF16)
+    disp[...] = dot(table, own_normed).astype(BF16)
+
+    def x_at(cc, yy):
+        return xrows.at[at(cc * 2 + yy, rows), :]
+
+    def x_part(cc, yy, e):
+        return xrows.at[pl.ds(pl.multiple_of((cc * 2 + yy) * rows + e * cap, cap), cap), :]
+
+    for k in range(1, n_ep):
+        send(disp.at[at(peer(k), cap), :], x_part(c, y, ep), d_ssem.at[k], d_rsem.at[k], dev(rep, peer(k)))
+    x_part(c, y, ep)[...] = disp[at(ep, cap), :]
+
+    send(n_at(c, x, y), n_at(c, x, y), n_ssem.at[0], n_rsem.at[0], x_dev)
+    send(n_at(c, x, y), n_at(c, x, y), n_ssem.at[1], n_rsem.at[1], y_dev)
+    send(n_at(c, x, y), n_at(c, x, y), n_ssem.at[2], n_rsem.at[2], core_dev)
+
+    def w1_at(s):
+        return w1.at[at(s, cols), :]
+
+    def w2_at(s):
+        return w2.at[s]
+
+    inner = (z > 0) & (z < PLANES - 1)
+
+    def line_start(piece, ssem, rsem):
+        @pl.when(z < PLANES - 1)
+        def _():
+            remote(piece(z), piece(z), ssem.at[0, z], rsem.at[z], up_dev).start()
+
+        @pl.when(z > 0)
+        def _():
+            remote(piece(z), piece(z), ssem.at[1, z], rsem.at[z], down_dev).start()
+
+    def order(j):
+        flip = z >= PLANES // 2
+        mine = jnp.where(flip, PLANES - 1 - z, z)
+        s = 1 - mine if j == 0 else j + 1
+        return jnp.where(flip, PLANES - 1 - s, s)
+
+    def line_step(piece, ssem, rsem, j):
+        s = order(j)
+        arrived(piece(s), ssem.at[0, s], rsem.at[s])
+
+        @pl.when(inner & (s < z))
+        def _():
+            remote(piece(s), piece(s), ssem.at[0, s], rsem.at[s], up_dev).start()
+
+        @pl.when(inner & (s > z))
+        def _():
+            remote(piece(s), piece(s), ssem.at[1, s], rsem.at[s], down_dev).start()
+
+        return s
+
+    def line_end(piece, ssem, rsem):
+        @pl.when(z < PLANES - 1)
+        def _():
+            remote(piece(z), piece(z), ssem.at[0, z], rsem.at[z], up_dev).wait_send()
+
+        @pl.when(z > 0)
+        def _():
+            remote(piece(z), piece(z), ssem.at[1, z], rsem.at[z], down_dev).wait_send()
+
+        for j in range(PLANES - 1):
+            s = order(j)
+
+            @pl.when(inner & (s < z))
+            def _():
+                remote(piece(s), piece(s), ssem.at[0, s], rsem.at[s], up_dev).wait_send()
+
+            @pl.when(inner & (s > z))
+            def _():
+                remote(piece(s), piece(s), ssem.at[1, s], rsem.at[s], down_dev).wait_send()
+
+    own_w1.wait()
+    arrived(w1.at[at(ep + 1 - 2 * x, chunk), :], wx_ssem.at[0], wx_rsem.at[0])
+    line_start(w1_at, w1_ssem, w1_rsem)
+
+    arrived(n_at(c, 1 - x, y), n_ssem.at[0], n_rsem.at[0])
+    send(n_at(c, 1 - x, y), n_at(c, 1 - x, y), n_ssem.at[3], n_rsem.at[3], y_dev)
+    send(n_at(c, 1 - x, y), n_at(c, 1 - x, y), n_ssem.at[4], n_rsem.at[4], core_dev)
+    for k in range(1, n_ep):
+        arrived(x_part(c, y, peer(n_ep - k)), d_ssem.at[k], d_rsem.at[k])
+    send(x_at(c, y), x_at(c, y), x_ssem.at[0], x_rsem.at[0], y_dev)
+    send(x_at(c, y), x_at(c, y), x_ssem.at[1], x_rsem.at[1], core_dev)
+    line_step(w1_at, w1_ssem, w1_rsem, 0)
+    own_w2.wait()
+    arrived(w2.at[z, :, at(1 - x, chunk)], wx_ssem.at[1], wx_rsem.at[1])
+    line_start(w2_at, w2_ssem, w2_rsem)
+    arrived(n_at(c, x, 1 - y), n_ssem.at[1], n_rsem.at[1])
+    send(n_at(c, x, 1 - y), n_at(c, x, 1 - y), n_ssem.at[5], n_rsem.at[5], core_dev)
+    arrived(x_at(c, 1 - y), x_ssem.at[0], x_rsem.at[0])
+    send(x_at(c, 1 - y), x_at(c, 1 - y), x_ssem.at[2], x_rsem.at[2], core_dev)
+    arrived(n_at(c, 1 - x, 1 - y), n_ssem.at[3], n_rsem.at[3])
+    send(n_at(c, 1 - x, 1 - y), n_at(c, 1 - x, 1 - y), n_ssem.at[6], n_rsem.at[6], core_dev)
+    line_step(w1_at, w1_ssem, w1_rsem, 1)
+
+    arrived(x_at(1 - c, y), x_ssem.at[1], x_rsem.at[1])
+    arrived(x_at(1 - c, 1 - y), x_ssem.at[2], x_rsem.at[2])
+    load_in.wait()
+
+    @pl.loop(0, ehid.shape[1] // 256)
+    def _(i):
+        ehid[:, at(i, 256)] = gelu(dot(xrows[...], ein[:, at(i, 256)])).astype(BF16)
+
+    line_step(w1_at, w1_ssem, w1_rsem, 2)
+    load_out.wait()
+
+    @pl.loop(0, width // 256)
+    def _(i):
+        er_send[:, at(i, 256)] = dot(ehid[at(1 - c, 2 * rows), :], eout[:, at(i, 256)]).astype(BF16)
+        er_keep[:, at(i, 256)] = dot(ehid[at(c, 2 * rows), :], eout[:, at(i, 256)])
+
+    send(er_send, er_recv, e_ssem.at[0], e_rsem.at[0], core_dev)
+    line_step(w2_at, w2_ssem, w2_rsem, 0)
+
+    arrived(n_at(1 - c, x, y), n_ssem.at[2], n_rsem.at[2])
+    arrived(n_at(1 - c, 1 - x, y), n_ssem.at[4], n_rsem.at[4])
+    arrived(n_at(1 - c, x, 1 - y), n_ssem.at[5], n_rsem.at[5])
+    arrived(n_at(1 - c, 1 - x, 1 - y), n_ssem.at[6], n_rsem.at[6])
+
+    @pl.loop(0, normed.shape[0] // 256)
+    def _(i):
+        rhid[at(i, 256), :] = gelu(dot(normed[at(i, 256), :], w1[...])).astype(BF16)
+
+    arrived(er_recv, e_ssem.at[0], e_rsem.at[0])
+    ey_send[...] = (er_keep[at(1 - y, rows), :] + er_recv[at(1 - y, rows), :].astype(F32)).astype(BF16)
+    send(ey_send, ey_recv, e_ssem.at[1], e_rsem.at[1], y_dev)
+    ey_keep[...] = er_keep[at(y, rows), :] + er_recv[at(y, rows), :].astype(F32)
+
+    def stage_a(s):
+        pc_send[s] = dot(rhid[at(1 - c, 4 * rows), :], w2[s]).astype(BF16)
+        send(pc_send.at[s], pc_recv.at[s], r_ssem.at[0, s], r_rsem.at[0, s], core_dev)
+        pc_keep[s] = dot(rhid[at(c, 4 * rows), :], w2[s])
+
+    def stage_b(s):
+        arrived(pc_recv.at[s], r_ssem.at[0, s], r_rsem.at[0, s])
+        away, stay = at(1 - x, 2 * rows), at(x, 2 * rows)
+        px_send[s] = (pc_keep[s, away, :] + pc_recv[s, away, :].astype(F32)).astype(BF16)
+        send(px_send.at[s], px_recv.at[s], r_ssem.at[1, s], r_rsem.at[1, s], x_dev)
+        px_keep[s] = pc_keep[s, stay, :] + pc_recv[s, stay, :].astype(F32)
+
+    def stage_c(s):
+        arrived(px_recv.at[s], r_ssem.at[1, s], r_rsem.at[1, s])
+        away, stay = at(1 - y, rows), at(y, rows)
+        py_send[s] = (px_keep[s, away, :] + px_recv[s, away, :].astype(F32)).astype(BF16)
+        send(py_send.at[s], py_recv.at[s], r_ssem.at[2, s], r_rsem.at[2, s], y_dev)
+        py_keep[s] = px_keep[s, stay, :] + px_recv[s, stay, :].astype(F32)
+
+    def stage_d(s):
+        arrived(py_recv.at[s], r_ssem.at[2, s], r_rsem.at[2, s])
+        res[s] = py_keep[s] + py_recv[s].astype(F32)
+
+    s0, s1, s2, s3 = z, order(0), order(1), order(2)
+    stage_a(s0)
+    stage_a(s1)
+    stage_b(s0)
+
+    arrived(ey_recv, e_ssem.at[1], e_rsem.at[1])
+    eb_send[...] = (ey_keep[...] + ey_recv[...].astype(F32)).astype(BF16)
+    for k in range(1, n_ep):
+        send(
+            eb_send.at[at(peer(k), cap), :], back.at[at(ep, cap), :],
+            b_ssem.at[k], b_rsem.at[k], dev(rep, peer(k)),
+        )
+    back[at(ep, cap), :] = eb_send[at(ep, cap), :]
+
+    line_step(w2_at, w2_ssem, w2_rsem, 1)
+    stage_a(s2)
+    stage_b(s1)
+    stage_c(s0)
+    stage_b(s2)
+    line_step(w2_at, w2_ssem, w2_rsem, 2)
+    stage_a(s3)
+    stage_c(s1)
+    stage_d(s0)
+    stage_b(s3)
+    stage_c(s2)
+    stage_d(s1)
+
+    for k in range(1, n_ep):
+        arrived(back.at[at(peer(n_ep - k), cap), :], b_ssem.at[k], b_rsem.at[k])
+    same = lax.broadcasted_iota(jnp.int32, (rows, rows), 0) == lax.broadcasted_iota(
+        jnp.int32, (rows, rows), 1
+    )
+    gate = jnp.sum(jnp.where(same, gates[...], 0.0), axis=1, keepdims=True)
+    picked = lax.dot_general(
+        table, back[...], (((0,), (0,)), ((), ())), preferred_element_type=F32
+    )
+    ey_keep[...] = tokens[...].astype(F32) + gate * picked
+
+    stage_c(s3)
+    stage_d(s2)
+    stage_d(s3)
+    for s in range(PLANES):
+        columns = pl.ds(s * cols, cols)
+        out[:, columns] = (ey_keep[:, columns] + res[s]).astype(BF16)
+
+    for copy in sent:
+        copy.wait_send()
+    line_end(w1_at, w1_ssem, w1_rsem)
+    line_end(w2_at, w2_ssem, w2_rsem)
+
+
+def one_kernel(
+    tokens, norm_gain, gates, expert_ids, slots, dropped, res_in, res_out, expert_in, expert_out
+):
+    rows, width = tokens.shape
+    chunk = res_in.shape[0]
+    half = res_in.shape[1] // 2
+    cols = 2 * chunk
+    units = expert_in.shape[2]
+    vmem = pl.BlockSpec(memory_space=pltpu.VMEM)
+    hbm = pl.BlockSpec(memory_space=pl.ANY)
+    dma = pltpu.SemaphoreType.DMA
+    scratch = [
+        pltpu.VMEM((width, half), BF16),
+        pltpu.VMEM((PLANES, half, cols), BF16),
+        pltpu.VMEM((width, units), BF16),
+        pltpu.VMEM((units, width), BF16),
+        pltpu.VMEM((8 * rows, width), BF16),
+        pltpu.VMEM((4 * rows, width), BF16),
+        pltpu.VMEM((rows, width), BF16),
+        pltpu.VMEM((4 * rows, units), BF16),
+        pltpu.VMEM((2 * rows, width), BF16),
+        pltpu.VMEM((2 * rows, width), F32),
+        pltpu.VMEM((2 * rows, width), BF16),
+        pltpu.VMEM((rows, width), BF16),
+        pltpu.VMEM((rows, width), F32),
+        pltpu.VMEM((rows, width), BF16),
+        pltpu.VMEM((rows, width), BF16),
+        pltpu.VMEM((rows, width), BF16),
+        pltpu.VMEM((8 * rows, half), BF16),
+    ]
+    for part in (4, 2, 1):
+        scratch += [
+            pltpu.VMEM((PLANES, part * rows, cols), BF16),
+            pltpu.VMEM((PLANES, part * rows, cols), F32),
+            pltpu.VMEM((PLANES, part * rows, cols), BF16),
+        ]
+    scratch += [pltpu.VMEM((PLANES, rows, cols), F32)]
+    scratch += [
+        dma((4,)), dma((2,)), dma((2,)),
+        dma((2, PLANES)), dma((PLANES,)), dma((2, PLANES)), dma((PLANES,)),
+        dma((7,)), dma((7,)), dma((8,)), dma((8,)), dma((3,)), dma((3,)),
+        dma((2,)), dma((2,)), dma((8,)), dma((8,)), dma((3, PLANES)), dma((3, PLANES)),
+    ]
+    return pl.pallas_call(
+        layer_kernel,
+        out_shape=jax.ShapeDtypeStruct((rows, width), BF16),
+        in_specs=[vmem] * 6 + [hbm] * 4,
+        out_specs=vmem,
+        scratch_shapes=scratch,
+        compiler_params=pltpu.CompilerParams(
+            collective_id=0, has_side_effects=True, vmem_limit_bytes=60 * 1024 * 1024
+        ),
+    )(
+        tokens, norm_gain.reshape(1, -1), gates.reshape(1, -1), expert_ids.reshape(1, -1),
+        slots.reshape(1, -1), dropped.reshape(1, -1), res_in, res_out,
+        expert_in.reshape(expert_in.shape[1:]), expert_out.reshape(expert_out.shape[1:]),
+    )
 
 
 def rms_norm(tokens, norm_gain):
@@ -67,8 +431,9 @@
 
 
 def solution(mesh):
+    planes = mesh.shape["rep"] == 4 and mesh.shape["ep"] == 2 * PLANES
     return jax.shard_map(
-        on_device,
+        one_kernel if planes else on_device,
         mesh=mesh,
         in_specs=(
             P(("rep", "ep"), None),

time: 361 us -> 136 us (0.38)
  waiting for transfers between devices: 277 us -> 0 us
  Pallas kernels: 0 us -> 134 us
  matrix products: 23.8 us -> 0 us
  blocking collectives: 16.3 us -> 0 us
  between operations: 13.2 us -> 0.01 us
  other arithmetic: 13.1 us -> 0 us
  starting transfers between devices: 9.45 us -> 0 us
  local copies, waits for them, and re-layouts: 7.62 us -> 1.88 us
    all_gather x3 -> x0, waiting for transfers between devices: 184 us -> none  [the longest x1 102 us: on_device(): weight_out = lax.all_gather(res_out, 'ep', axis=1, tiled=True)]
    pallas_call x0 -> x1, Pallas kernels: none -> 134 us  [one_kernel(): pl.pallas_call(layer_kernel, out_shape=jax.ShapeDtypeStruct((rows, width)...]
    all_to_all x2 -> x0, waiting for transfers between devices: 47.4 us -> none  [the longest x1 47.4 us: on_device(): lax.all_to_all(result.reshape(block.shape[0], block.shape[1], width).asty...]
    reduce_scatter x2 -> x0, waiting for transfers between devices: 43.7 us -> none  [the longest x1 43.7 us: on_device(): lax.psum_scatter(partial_rows, 'rep', scatter_dimension=0, tiled=True)]
    dot_general x4 -> x0, matrix products: 23.8 us -> none  [the longest x1 10.9 us: on_device(): jnp.dot(hidden, weight_out, preferred_element_type=jnp.float32)]
    all_gather x3 -> x0, blocking collectives: 16.3 us -> none  [the longest x1 5.98 us: on_device(): lax.all_gather(keep, 'rep', axis=0, tiled=True)]
    all_to_all x2 -> x0, starting transfers between devices: 9.11 us -> none  [the longest x1 5.51 us: on_device(): lax.all_to_all(buffer, 'ep', split_axis=0, concat_axis=0, tiled=True)]
    gather x1 -> x0, local copies, waits for them, and re-layouts: 7.6 us -> none  [on_device(): jnp.take(back.reshape(-1, width), jnp.where(keep_all == 1, target, 0), ax...]
  transfers between devices with their start and end apart: 7 -> 0, of which waited for: 5 -> 0; matrix products, arithmetic and copies ran while one was open for 11% -> 0% of each run, Pallas kernels for 0% -> 0%
where the time goes in v1:
time: 136 us
  Pallas kernels  134 us (99%)
  local copies, waits for them, and re-layouts  1.88 us (1%)
    pallas_call x1, Pallas kernels, one_kernel(): pl.pallas_call(layer_kernel, out_shape=jax.ShapeDtypeStruct((rows, width)...  134 us

profile of v1, /device:TPU:0, one launch (start us, length us, event | category | flops | bytes accessed | tf_op | source)
XLA Modules:
  0.0 135.9 jit_solution(7061021048380764915)
XLA Ops:
  0.0 134.0 %shard_map.100 = bf16[128,2048]{1,0:T(8,128)(2,1)} custom-call(bf16[128,2048]{1,0:T(8,128)(2,1)} %tokens.1, f32[1,2048]{1,0:T(1,128)} %bitcast.9, f32[1,128]{1,0:T(1,128)} %bitcast.10, s32[1,128]{1,0:T(1,128)} %bitcast.11, s32[1,128]{1,0:T(1,128)} %bitcast.12, s32[1,128]{1,0:T(1,128)} %bitcast.13, bf16[256,1024]{1,0:T(8,128)(2,1)} %res_in.1, ...), custom_call_target="tpu_custom_call" | custom-call | tf_op jit(solution)/shard_map/pallas_call | solution.py:355
  134.0 1.9 %copy.12 = bf16[128,2048]{1,0:T(8,128)(2,1)} copy(bf16[128,2048]{1,0:T(8,128)(2,1)} %shard_map.100) | data formatting | bytes 1048576

commit v2 on v1

--- a/solution.py
+++ b/solution.py
@@ -89,10 +89,6 @@
     pl.semaphore_wait(barrier, n_ep + 1)
 
     send(res_in.at[:, at(1 - x, half)], w1.at[at(ep, chunk), :], wx_ssem.at[0], wx_rsem.at[0], x_dev)
-    send(
-        res_out.at[at(1 - x, half), :], w2.at[z, :, at(x, chunk)],
-        wx_ssem.at[1], wx_rsem.at[1], x_dev,
-    )
 
     values = tokens[...].astype(F32)
     scale = lax.rsqrt(jnp.mean(values * values, axis=-1, keepdims=True) + 1e-06)
@@ -118,7 +114,6 @@
         send(disp.at[at(peer(k), cap), :], x_part(c, y, ep), d_ssem.at[k], d_rsem.at[k], dev(rep, peer(k)))
     x_part(c, y, ep)[...] = disp[at(ep, cap), :]
 
-    send(n_at(c, x, y), n_at(c, x, y), n_ssem.at[0], n_rsem.at[0], x_dev)
     send(n_at(c, x, y), n_at(c, x, y), n_ssem.at[1], n_rsem.at[1], y_dev)
     send(n_at(c, x, y), n_at(c, x, y), n_ssem.at[2], n_rsem.at[2], core_dev)
 
@@ -145,9 +140,19 @@
         s = 1 - mine if j == 0 else j + 1
         return jnp.where(flip, PLANES - 1 - s, s)
 
+    def line_wait(piece, ssem, rsem, j):
+        s = order(j)
+
+        @pl.when(jnp.logical_not(inner))
+        def _():
+            arrived(piece(s), ssem.at[0, s], rsem.at[s])
+
     def line_step(piece, ssem, rsem, j):
         s = order(j)
-        arrived(piece(s), ssem.at[0, s], rsem.at[s])
+
+        @pl.when(inner)
+        def _():
+            arrived(piece(s), ssem.at[0, s], rsem.at[s])
 
         @pl.when(inner & (s < z))
         def _():
@@ -156,8 +161,6 @@
         @pl.when(inner & (s > z))
         def _():
             remote(piece(s), piece(s), ssem.at[1, s], rsem.at[s], down_dev).start()
-
-        return s
 
     def line_end(piece, ssem, rsem):
         @pl.when(z < PLANES - 1)
@@ -183,24 +186,28 @@
     arrived(w1.at[at(ep + 1 - 2 * x, chunk), :], wx_ssem.at[0], wx_rsem.at[0])
     line_start(w1_at, w1_ssem, w1_rsem)
 
-    arrived(n_at(c, 1 - x, y), n_ssem.at[0], n_rsem.at[0])
-    send(n_at(c, 1 - x, y), n_at(c, 1 - x, y), n_ssem.at[3], n_rsem.at[3], y_dev)
-    send(n_at(c, 1 - x, y), n_at(c, 1 - x, y), n_ssem.at[4], n_rsem.at[4], core_dev)
+    send(n_at(c, x, y), n_at(c, x, y), n_ssem.at[0], n_rsem.at[0], x_dev)
+    send(
+        res_out.at[at(1 - x, half), :], w2.at[z, :, at(x, chunk)],
+        wx_ssem.at[1], wx_rsem.at[1], x_dev,
+    )
     for k in range(1, n_ep):
         arrived(x_part(c, y, peer(n_ep - k)), d_ssem.at[k], d_rsem.at[k])
     send(x_at(c, y), x_at(c, y), x_ssem.at[0], x_rsem.at[0], y_dev)
     send(x_at(c, y), x_at(c, y), x_ssem.at[1], x_rsem.at[1], core_dev)
+    arrived(n_at(c, x, 1 - y), n_ssem.at[1], n_rsem.at[1])
+    send(n_at(c, x, 1 - y), n_at(c, x, 1 - y), n_ssem.at[5], n_rsem.at[5], core_dev)
     line_step(w1_at, w1_ssem, w1_rsem, 0)
+    line_step(w1_at, w1_ssem, w1_rsem, 1)
+    arrived(n_at(c, 1 - x, y), n_ssem.at[0], n_rsem.at[0])
+    send(n_at(c, 1 - x, y), n_at(c, 1 - x, y), n_ssem.at[3], n_rsem.at[3], y_dev)
+    send(n_at(c, 1 - x, y), n_at(c, 1 - x, y), n_ssem.at[4], n_rsem.at[4], core_dev)
     own_w2.wait()
     arrived(w2.at[z, :, at(1 - x, chunk)], wx_ssem.at[1], wx_rsem.at[1])
     line_start(w2_at, w2_ssem, w2_rsem)
-    arrived(n_at(c, x, 1 - y), n_ssem.at[1], n_rsem.at[1])
-    send(n_at(c, x, 1 - y), n_at(c, x, 1 - y), n_ssem.at[5], n_rsem.at[5], core_dev)
     arrived(x_at(c, 1 - y), x_ssem.at[0], x_rsem.at[0])
     send(x_at(c, 1 - y), x_at(c, 1 - y), x_ssem.at[2], x_rsem.at[2], core_dev)
-    arrived(n_at(c, 1 - x, 1 - y), n_ssem.at[3], n_rsem.at[3])
-    send(n_at(c, 1 - x, 1 - y), n_at(c, 1 - x, 1 - y), n_ssem.at[6], n_rsem.at[6], core_dev)
-    line_step(w1_at, w1_ssem, w1_rsem, 1)
+    line_step(w1_at, w1_ssem, w1_rsem, 2)
 
     arrived(x_at(1 - c, y), x_ssem.at[1], x_rsem.at[1])
     arrived(x_at(1 - c, 1 - y), x_ssem.at[2], x_rsem.at[2])
@@ -210,7 +217,6 @@
     def _(i):
         ehid[:, at(i, 256)] = gelu(dot(xrows[...], ein[:, at(i, 256)])).astype(BF16)
 
-    line_step(w1_at, w1_ssem, w1_rsem, 2)
     load_out.wait()
 
     @pl.loop(0, width // 256)
@@ -219,21 +225,24 @@
         er_keep[:, at(i, 256)] = dot(ehid[at(c, 2 * rows), :], eout[:, at(i, 256)])
 
     send(er_send, er_recv, e_ssem.at[0], e_rsem.at[0], core_dev)
-    line_step(w2_at, w2_ssem, w2_rsem, 0)
-
+    arrived(er_recv, e_ssem.at[0], e_rsem.at[0])
+    ey_send[...] = (er_keep[at(1 - y, rows), :] + er_recv[at(1 - y, rows), :].astype(F32)).astype(BF16)
+    send(ey_send, ey_recv, e_ssem.at[1], e_rsem.at[1], y_dev)
+    ey_keep[...] = er_keep[at(y, rows), :] + er_recv[at(y, rows), :].astype(F32)
+
+    arrived(n_at(c, 1 - x, 1 - y), n_ssem.at[3], n_rsem.at[3])
+    send(n_at(c, 1 - x, 1 - y), n_at(c, 1 - x, 1 - y), n_ssem.at[6], n_rsem.at[6], core_dev)
     arrived(n_at(1 - c, x, y), n_ssem.at[2], n_rsem.at[2])
     arrived(n_at(1 - c, 1 - x, y), n_ssem.at[4], n_rsem.at[4])
     arrived(n_at(1 - c, x, 1 - y), n_ssem.at[5], n_rsem.at[5])
     arrived(n_at(1 - c, 1 - x, 1 - y), n_ssem.at[6], n_rsem.at[6])
 
+    for j in range(PLANES - 1):
+        line_wait(w1_at, w1_ssem, w1_rsem, j)
+
     @pl.loop(0, normed.shape[0] // 256)
     def _(i):
         rhid[at(i, 256), :] = gelu(dot(normed[at(i, 256), :], w1[...])).astype(BF16)
-
-    arrived(er_recv, e_ssem.at[0], e_rsem.at[0])
-    ey_send[...] = (er_keep[at(1 - y, rows), :] + er_recv[at(1 - y, rows), :].astype(F32)).astype(BF16)
-    send(ey_send, ey_recv, e_ssem.at[1], e_rsem.at[1], y_dev)
-    ey_keep[...] = er_keep[at(y, rows), :] + er_recv[at(y, rows), :].astype(F32)
 
     def stage_a(s):
         pc_send[s] = dot(rhid[at(1 - c, 4 * rows), :], w2[s]).astype(BF16)
@@ -259,10 +268,9 @@
         res[s] = py_keep[s] + py_recv[s].astype(F32)
 
     s0, s1, s2, s3 = z, order(0), order(1), order(2)
+    line_step(w2_at, w2_ssem, w2_rsem, 0)
+    line_step(w2_at, w2_ssem, w2_rsem, 1)
     stage_a(s0)
-    stage_a(s1)
-    stage_b(s0)
-
     arrived(ey_recv, e_ssem.at[1], e_rsem.at[1])
     eb_send[...] = (ey_keep[...] + ey_recv[...].astype(F32)).astype(BF16)
     for k in range(1, n_ep):
@@ -272,19 +280,17 @@
         )
     back[at(ep, cap), :] = eb_send[at(ep, cap), :]
 
-    line_step(w2_at, w2_ssem, w2_rsem, 1)
+    stage_b(s0)
+    line_wait(w2_at, w2_ssem, w2_rsem, 0)
+    stage_a(s1)
+    stage_b(s1)
+    line_step(w2_at, w2_ssem, w2_rsem, 2)
+    stage_c(s0)
+    line_wait(w2_at, w2_ssem, w2_rsem, 1)
     stage_a(s2)
-    stage_b(s1)
-    stage_c(s0)
     stage_b(s2)
-    line_step(w2_at, w2_ssem, w2_rsem, 2)
-    stage_a(s3)
     stage_c(s1)
     stage_d(s0)
-    stage_b(s3)
-    stage_c(s2)
-    stage_d(s1)
-
     for k in range(1, n_ep):
         arrived(back.at[at(peer(n_ep - k), cap), :], b_ssem.at[k], b_rsem.at[k])
     same = lax.broadcasted_iota(jnp.int32, (rows, rows), 0) == lax.broadcasted_iota(
@@ -296,8 +302,13 @@
     )
     ey_keep[...] = tokens[...].astype(F32) + gate * picked
 
+    stage_c(s2)
+    stage_d(s1)
+    line_wait(w2_at, w2_ssem, w2_rsem, 2)
+    stage_a(s3)
+    stage_b(s3)
+    stage_d(s2)
     stage_c(s3)
-    stage_d(s2)
     stage_d(s3)
     for s in range(PLANES):
         columns = pl.ds(s * cols, cols)

time: 136 us -> 115 us (0.85)
  Pallas kernels: 134 us -> 113 us
    pallas_call x1, Pallas kernels: 134 us -> 113 us  [one_kernel(): pl.pallas_call(layer_kernel, out_shape=jax.ShapeDtypeStruct((rows, width)...]
where the time goes in v2:
time: 115 us
  Pallas kernels  113 us (98%)
  local copies, waits for them, and re-layouts  1.88 us (2%)
    pallas_call x1, Pallas kernels, one_kernel(): pl.pallas_call(layer_kernel, out_shape=jax.ShapeDtypeStruct((rows, width)...  113 us

profile of v2, /device:TPU:0, one launch (start us, length us, event | category | flops | bytes accessed | tf_op | source)
XLA Modules:
  0.0 115.1 jit_solution(2938547966423878134)
XLA Ops:
  0.0 113.2 %shard_map.100 = bf16[128,2048]{1,0:T(8,128)(2,1)} custom-call(bf16[128,2048]{1,0:T(8,128)(2,1)} %tokens.1, f32[1,2048]{1,0:T(1,128)} %bitcast.9, f32[1,128]{1,0:T(1,128)} %bitcast.10, s32[1,128]{1,0:T(1,128)} %bitcast.11, s32[1,128]{1,0:T(1,128)} %bitcast.12, s32[1,128]{1,0:T(1,128)} %bitcast.13, bf16[256,1024]{1,0:T(8,128)(2,1)} %res_in.1, ...), custom_call_target="tpu_custom_call" | custom-call | tf_op jit(solution)/shard_map/pallas_call | solution.py:366
  113.2 1.9 %copy.12 = bf16[128,2048]{1,0:T(8,128)(2,1)} copy(bf16[128,2048]{1,0:T(8,128)(2,1)} %shard_map.100) | data formatting | bytes 1048576

commit v3 on v2

--- a/solution.py
+++ b/solution.py
@@ -90,49 +90,26 @@
 
     send(res_in.at[:, at(1 - x, half)], w1.at[at(ep, chunk), :], wx_ssem.at[0], wx_rsem.at[0], x_dev)
 
-    values = tokens[...].astype(F32)
-    scale = lax.rsqrt(jnp.mean(values * values, axis=-1, keepdims=True) + 1e-06)
-    own_normed = (values * scale * gain[...]).astype(BF16)
-
-    def n_at(cc, xx, yy):
-        return normed.at[at(cc * 4 + xx * 2 + yy, rows), :]
-
-    normed[at(c * 4 + x * 2 + y, rows), :] = own_normed
-
-    target = ids[...] * cap + slots[...]
-    places = lax.broadcasted_iota(jnp.int32, (n_ep * cap, rows), 0)
-    table = jnp.where((places == target) & (dropped[...] == 0), 1.0, 0.0).astype(BF16)
-    disp[...] = dot(table, own_normed).astype(BF16)
-
-    def x_at(cc, yy):
-        return xrows.at[at(cc * 2 + yy, rows), :]
-
-    def x_part(cc, yy, e):
-        return xrows.at[pl.ds(pl.multiple_of((cc * 2 + yy) * rows + e * cap, cap), cap), :]
-
-    for k in range(1, n_ep):
-        send(disp.at[at(peer(k), cap), :], x_part(c, y, ep), d_ssem.at[k], d_rsem.at[k], dev(rep, peer(k)))
-    x_part(c, y, ep)[...] = disp[at(ep, cap), :]
-
-    send(n_at(c, x, y), n_at(c, x, y), n_ssem.at[1], n_rsem.at[1], y_dev)
-    send(n_at(c, x, y), n_at(c, x, y), n_ssem.at[2], n_rsem.at[2], core_dev)
-
-    def w1_at(s):
-        return w1.at[at(s, cols), :]
-
-    def w2_at(s):
-        return w2.at[s]
+    def w1_at(s, h):
+        return w1.at[at(2 * s + h, chunk), :]
+
+    def w2_at(s, h):
+        return w2.at[s, :, at(h, chunk)]
 
     inner = (z > 0) & (z < PLANES - 1)
 
-    def line_start(piece, ssem, rsem):
+    def line_copy(piece, ssem, rsem, s, h, way):
+        device = down_dev if way else up_dev
+        return remote(piece(s, h), piece(s, h), ssem.at[way, h, s], rsem.at[h, s], device)
+
+    def line_start(piece, ssem, rsem, h):
         @pl.when(z < PLANES - 1)
         def _():
-            remote(piece(z), piece(z), ssem.at[0, z], rsem.at[z], up_dev).start()
+            line_copy(piece, ssem, rsem, z, h, 0).start()
 
         @pl.when(z > 0)
         def _():
-            remote(piece(z), piece(z), ssem.at[1, z], rsem.at[z], down_dev).start()
+            line_copy(piece, ssem, rsem, z, h, 1).start()
 
     def order(j):
         flip = z >= PLANES // 2
@@ -140,51 +117,82 @@
         s = 1 - mine if j == 0 else j + 1
         return jnp.where(flip, PLANES - 1 - s, s)
 
-    def line_wait(piece, ssem, rsem, j):
+    def line_wait(piece, ssem, rsem, j, halves=(0, 1)):
         s = order(j)
 
         @pl.when(jnp.logical_not(inner))
         def _():
-            arrived(piece(s), ssem.at[0, s], rsem.at[s])
+            for h in halves:
+                line_copy(piece, ssem, rsem, s, h, 0).wait_recv()
 
     def line_step(piece, ssem, rsem, j):
         s = order(j)
-
-        @pl.when(inner)
-        def _():
-            arrived(piece(s), ssem.at[0, s], rsem.at[s])
-
-        @pl.when(inner & (s < z))
-        def _():
-            remote(piece(s), piece(s), ssem.at[0, s], rsem.at[s], up_dev).start()
-
-        @pl.when(inner & (s > z))
-        def _():
-            remote(piece(s), piece(s), ssem.at[1, s], rsem.at[s], down_dev).start()
-
-    def line_end(piece, ssem, rsem):
-        @pl.when(z < PLANES - 1)
-        def _():
-            remote(piece(z), piece(z), ssem.at[0, z], rsem.at[z], up_dev).wait_send()
-
-        @pl.when(z > 0)
-        def _():
-            remote(piece(z), piece(z), ssem.at[1, z], rsem.at[z], down_dev).wait_send()
-
-        for j in range(PLANES - 1):
-            s = order(j)
+        for h in (0, 1):
+            @pl.when(inner)
+            def _():
+                line_copy(piece, ssem, rsem, s, h, 0).wait_recv()
 
             @pl.when(inner & (s < z))
             def _():
-                remote(piece(s), piece(s), ssem.at[0, s], rsem.at[s], up_dev).wait_send()
+                line_copy(piece, ssem, rsem, s, h, 0).start()
 
             @pl.when(inner & (s > z))
             def _():
-                remote(piece(s), piece(s), ssem.at[1, s], rsem.at[s], down_dev).wait_send()
+                line_copy(piece, ssem, rsem, s, h, 1).start()
+
+    def line_end(piece, ssem, rsem):
+        for h in (0, 1):
+            @pl.when(z < PLANES - 1)
+            def _():
+                line_copy(piece, ssem, rsem, z, h, 0).wait_send()
+
+            @pl.when(z > 0)
+            def _():
+                line_copy(piece, ssem, rsem, z, h, 1).wait_send()
+
+            for j in range(PLANES - 1):
+                s = order(j)
+
+                @pl.when(inner & (s < z))
+                def _():
+                    line_copy(piece, ssem, rsem, s, h, 0).wait_send()
+
+                @pl.when(inner & (s > z))
+                def _():
+                    line_copy(piece, ssem, rsem, s, h, 1).wait_send()
 
     own_w1.wait()
+    line_start(w1_at, w1_ssem, w1_rsem, x)
+
+    values = tokens[...].astype(F32)
+    scale = lax.rsqrt(jnp.mean(values * values, axis=-1, keepdims=True) + 1e-06)
+    own_normed = (values * scale * gain[...]).astype(BF16)
+
+    def n_at(cc, xx, yy):
+        return normed.at[at(cc * 4 + xx * 2 + yy, rows), :]
+
+    normed[at(c * 4 + x * 2 + y, rows), :] = own_normed
+
+    target = ids[...] * cap + slots[...]
+    places = lax.broadcasted_iota(jnp.int32, (n_ep * cap, rows), 0)
+    table = jnp.where((places == target) & (dropped[...] == 0), 1.0, 0.0).astype(BF16)
+    disp[...] = dot(table, own_normed).astype(BF16)
+
+    def x_at(cc, yy):
+        return xrows.at[at(cc * 2 + yy, rows), :]
+
+    def x_part(cc, yy, e):
+        return xrows.at[pl.ds(pl.multiple_of((cc * 2 + yy) * rows + e * cap, cap), cap), :]
+
+    for k in range(1, n_ep):
+        send(disp.at[at(peer(k), cap), :], x_part(c, y, ep), d_ssem.at[k], d_rsem.at[k], dev(rep, peer(k)))
+    x_part(c, y, ep)[...] = disp[at(ep, cap), :]
+
+    send(n_at(c, x, y), n_at(c, x, y), n_ssem.at[1], n_rsem.at[1], y_dev)
+    send(n_at(c, x, y), n_at(c, x, y), n_ssem.at[2], n_rsem.at[2], core_dev)
+
     arrived(w1.at[at(ep + 1 - 2 * x, chunk), :], wx_ssem.at[0], wx_rsem.at[0])
-    line_start(w1_at, w1_ssem, w1_rsem)
+    line_start(w1_at, w1_ssem, w1_rsem, 1 - x)
 
     send(n_at(c, x, y), n_at(c, x, y), n_ssem.at[0], n_rsem.at[0], x_dev)
     send(
@@ -204,7 +212,8 @@
     send(n_at(c, 1 - x, y), n_at(c, 1 - x, y), n_ssem.at[4], n_rsem.at[4], core_dev)
     own_w2.wait()
     arrived(w2.at[z, :, at(1 - x, chunk)], wx_ssem.at[1], wx_rsem.at[1])
-    line_start(w2_at, w2_ssem, w2_rsem)
+    line_start(w2_at, w2_ssem, w2_rsem, 0)
+    line_start(w2_at, w2_ssem, w2_rsem, 1)
     arrived(x_at(c, 1 - y), x_ssem.at[0], x_rsem.at[0])
     send(x_at(c, 1 - y), x_at(c, 1 - y), x_ssem.at[2], x_rsem.at[2], core_dev)
     line_step(w1_at, w1_ssem, w1_rsem, 2)
@@ -244,33 +253,34 @@
     def _(i):
         rhid[at(i, 256), :] = gelu(dot(normed[at(i, 256), :], w1[...])).astype(BF16)
 
-    def stage_a(s):
-        pc_send[s] = dot(rhid[at(1 - c, 4 * rows), :], w2[s]).astype(BF16)
-        send(pc_send.at[s], pc_recv.at[s], r_ssem.at[0, s], r_rsem.at[0, s], core_dev)
-        pc_keep[s] = dot(rhid[at(c, 4 * rows), :], w2[s])
-
-    def stage_b(s):
-        arrived(pc_recv.at[s], r_ssem.at[0, s], r_rsem.at[0, s])
+    def stage_a(s, q, cs):
+        pc_send[s, :, cs] = dot(rhid[at(1 - c, 4 * rows), :], w2[s, :, cs]).astype(BF16)
+        send(pc_send.at[s, :, cs], pc_recv.at[s, :, cs], r_ssem.at[0, q], r_rsem.at[0, q], core_dev)
+        pc_keep[s, :, cs] = dot(rhid[at(c, 4 * rows), :], w2[s, :, cs])
+
+    def stage_b(s, q, cs):
+        arrived(pc_recv.at[s, :, cs], r_ssem.at[0, q], r_rsem.at[0, q])
         away, stay = at(1 - x, 2 * rows), at(x, 2 * rows)
-        px_send[s] = (pc_keep[s, away, :] + pc_recv[s, away, :].astype(F32)).astype(BF16)
-        send(px_send.at[s], px_recv.at[s], r_ssem.at[1, s], r_rsem.at[1, s], x_dev)
-        px_keep[s] = pc_keep[s, stay, :] + pc_recv[s, stay, :].astype(F32)
-
-    def stage_c(s):
-        arrived(px_recv.at[s], r_ssem.at[1, s], r_rsem.at[1, s])
+        px_send[s, :, cs] = (pc_keep[s, away, cs] + pc_recv[s, away, cs].astype(F32)).astype(BF16)
+        send(px_send.at[s, :, cs], px_recv.at[s, :, cs], r_ssem.at[1, q], r_rsem.at[1, q], x_dev)
+        px_keep[s, :, cs] = pc_keep[s, stay, cs] + pc_recv[s, stay, cs].astype(F32)
+
+    def stage_c(s, q, cs):
+        arrived(px_recv.at[s, :, cs], r_ssem.at[1, q], r_rsem.at[1, q])
         away, stay = at(1 - y, rows), at(y, rows)
-        py_send[s] = (px_keep[s, away, :] + px_recv[s, away, :].astype(F32)).astype(BF16)
-        send(py_send.at[s], py_recv.at[s], r_ssem.at[2, s], r_rsem.at[2, s], y_dev)
-        py_keep[s] = px_keep[s, stay, :] + px_recv[s, stay, :].astype(F32)
-
-    def stage_d(s):
-        arrived(py_recv.at[s], r_ssem.at[2, s], r_rsem.at[2, s])
-        res[s] = py_keep[s] + py_recv[s].astype(F32)
+        py_send[s, :, cs] = (px_keep[s, away, cs] + px_recv[s, away, cs].astype(F32)).astype(BF16)
+        send(py_send.at[s, :, cs], py_recv.at[s, :, cs], r_ssem.at[2, q], r_rsem.at[2, q], y_dev)
+        py_keep[s, :, cs] = px_keep[s, stay, cs] + px_recv[s, stay, cs].astype(F32)
+
+    def stage_d(s, q, cs):
+        arrived(py_recv.at[s, :, cs], r_ssem.at[2, q], r_rsem.at[2, q])
+        res[s, :, cs] = py_keep[s, :, cs] + py_recv[s, :, cs].astype(F32)
 
     s0, s1, s2, s3 = z, order(0), order(1), order(2)
+    whole, left, right = pl.ds(0, cols), pl.ds(0, chunk), pl.ds(chunk, chunk)
     line_step(w2_at, w2_ssem, w2_rsem, 0)
     line_step(w2_at, w2_ssem, w2_rsem, 1)
-    stage_a(s0)
+    stage_a(s0, s0, whole)
     arrived(ey_recv, e_ssem.at[1], e_rsem.at[1])
     eb_send[...] = (ey_keep[...] + ey_recv[...].astype(F32)).astype(BF16)
     for k in range(1, n_ep):
@@ -280,17 +290,17 @@
         )
     back[at(ep, cap), :] = eb_send[at(ep, cap), :]
 
-    stage_b(s0)
+    stage_b(s0, s0, whole)
     line_wait(w2_at, w2_ssem, w2_rsem, 0)
-    stage_a(s1)
-    stage_b(s1)
+    stage_a(s1, s1, whole)
+    stage_b(s1, s1, whole)
     line_step(w2_at, w2_ssem, w2_rsem, 2)
-    stage_c(s0)
+    stage_c(s0, s0, whole)
     line_wait(w2_at, w2_ssem, w2_rsem, 1)
-    stage_a(s2)
-    stage_b(s2)
-    stage_c(s1)
-    stage_d(s0)
+    stage_a(s2, s2, whole)
+    stage_b(s2, s2, whole)
+    stage_c(s1, s1, whole)
+    stage_d(s0, s0, whole)
     for k in range(1, n_ep):
         arrived(back.at[at(peer(n_ep - k), cap), :], b_ssem.at[k], b_rsem.at[k])
     same = lax.broadcasted_iota(jnp.int32, (rows, rows), 0) == lax.broadcasted_iota(
@@ -302,14 +312,19 @@
     )
     ey_keep[...] = tokens[...].astype(F32) + gate * picked
 
-    stage_c(s2)
-    stage_d(s1)
-    line_wait(w2_at, w2_ssem, w2_rsem, 2)
-    stage_a(s3)
-    stage_b(s3)
-    stage_d(s2)
-    stage_c(s3)
-    stage_d(s3)
+    stage_c(s2, s2, whole)
+    stage_d(s1, s1, whole)
+    line_wait(w2_at, w2_ssem, w2_rsem, 2, (0,))
+    stage_a(s3, s3, left)
+    stage_d(s2, s2, whole)
+    stage_b(s3, s3, left)
+    line_wait(w2_at, w2_ssem, w2_rsem, 2, (1,))
+    stage_a(s3, PLANES, right)
+    stage_b(s3, PLANES, right)
+    stage_c(s3, s3, left)
+    stage_c(s3, PLANES, right)
+    stage_d(s3, s3, left)
+    stage_d(s3, PLANES, right)
     for s in range(PLANES):
         columns = pl.ds(s * cols, cols)
         out[:, columns] = (ey_keep[:, columns] + res[s]).astype(BF16)
@@ -359,9 +374,9 @@
     scratch += [pltpu.VMEM((PLANES, rows, cols), F32)]
     scratch += [
         dma((4,)), dma((2,)), dma((2,)),
-        dma((2, PLANES)), dma((PLANES,)), dma((2, PLANES)), dma((PLANES,)),
+        dma((2, 2, PLANES)), dma((2, PLANES)), dma((2, 2, PLANES)), dma((2, PLANES)),
         dma((7,)), dma((7,)), dma((8,)), dma((8,)), dma((3,)), dma((3,)),
-        dma((2,)), dma((2,)), dma((8,)), dma((8,)), dma((3, PLANES)), dma((3, PLANES)),
+        dma((2,)), dma((2,)), dma((8,)), dma((8,)), dma((3, PLANES + 1)), dma((3, PLANES + 1)),
     ]
     return pl.pallas_call(
         layer_kernel,

time: 115 us -> 112 us (0.974)
  Pallas kernels: 113 us -> 110 us
    pallas_call x1, Pallas kernels: 113 us -> 110 us  [one_kernel(): pl.pallas_call(layer_kernel, out_shape=jax.ShapeDtypeStruct((rows, width)...]
where the time goes in v3:
time: 112 us
  Pallas kernels  110 us (98%)
  local copies, waits for them, and re-layouts  1.88 us (2%)
    pallas_call x1, Pallas kernels, one_kernel(): pl.pallas_call(layer_kernel, out_shape=jax.ShapeDtypeStruct((rows, width)...  110 us

profile of v3, /device:TPU:0, one launch (start us, length us, event | category | flops | bytes accessed | tf_op | source)
XLA Modules:
  0.0 112.0 jit_solution(4735113943088223397)
XLA Ops:
  0.0 110.1 %shard_map.100 = bf16[128,2048]{1,0:T(8,128)(2,1)} custom-call(bf16[128,2048]{1,0:T(8,128)(2,1)} %tokens.1, f32[1,2048]{1,0:T(1,128)} %bitcast.9, f32[1,128]{1,0:T(1,128)} %bitcast.10, s32[1,128]{1,0:T(1,128)} %bitcast.11, s32[1,128]{1,0:T(1,128)} %bitcast.12, s32[1,128]{1,0:T(1,128)} %bitcast.13, bf16[256,1024]{1,0:T(8,128)(2,1)} %res_in.1, ...), custom_call_target="tpu_custom_call" | custom-call | tf_op jit(solution)/shard_map/pallas_call | solution.py:381
  110.1 1.9 %copy.12 = bf16[128,2048]{1,0:T(8,128)(2,1)} copy(bf16[128,2048]{1,0:T(8,128)(2,1)} %shard_map.100) | data formatting | bytes 1048576

commit v4 on v3

--- a/solution.py
+++ b/solution.py
@@ -193,6 +193,8 @@
 
     arrived(w1.at[at(ep + 1 - 2 * x, chunk), :], wx_ssem.at[0], wx_rsem.at[0])
     line_start(w1_at, w1_ssem, w1_rsem, 1 - x)
+    own_w2.wait()
+    line_start(w2_at, w2_ssem, w2_rsem, x)
 
     send(n_at(c, x, y), n_at(c, x, y), n_ssem.at[0], n_rsem.at[0], x_dev)
     send(
@@ -210,10 +212,8 @@
     arrived(n_at(c, 1 - x, y), n_ssem.at[0], n_rsem.at[0])
     send(n_at(c, 1 - x, y), n_at(c, 1 - x, y), n_ssem.at[3], n_rsem.at[3], y_dev)
     send(n_at(c, 1 - x, y), n_at(c, 1 - x, y), n_ssem.at[4], n_rsem.at[4], core_dev)
-    own_w2.wait()
     arrived(w2.at[z, :, at(1 - x, chunk)], wx_ssem.at[1], wx_rsem.at[1])
-    line_start(w2_at, w2_ssem, w2_rsem, 0)
-    line_start(w2_at, w2_ssem, w2_rsem, 1)
+    line_start(w2_at, w2_ssem, w2_rsem, 1 - x)
     arrived(x_at(c, 1 - y), x_ssem.at[0], x_rsem.at[0])
     send(x_at(c, 1 - y), x_at(c, 1 - y), x_ssem.at[2], x_rsem.at[2], core_dev)
     line_step(w1_at, w1_ssem, w1_rsem, 2)

time: 112 us -> 109 us (0.973)
  Pallas kernels: 110 us -> 107 us
    pallas_call x1, Pallas kernels: 110 us -> 107 us  [one_kernel(): pl.pallas_call(layer_kernel, out_shape=jax.ShapeDtypeStruct((rows, width)...]
where the time goes in v4:
time: 109 us
  Pallas kernels  107 us (98%)
  local copies, waits for them, and re-layouts  1.88 us (2%)
    pallas_call x1, Pallas kernels, one_kernel(): pl.pallas_call(layer_kernel, out_shape=jax.ShapeDtypeStruct((rows, width)...  107 us

profile of v4, /device:TPU:0, one launch (start us, length us, event | category | flops | bytes accessed | tf_op | source)
XLA Modules:
  0.0 109.0 jit_solution(8649924611746843968)
XLA Ops:
  0.0 107.2 %shard_map.100 = bf16[128,2048]{1,0:T(8,128)(2,1)} custom-call(bf16[128,2048]{1,0:T(8,128)(2,1)} %tokens.1, f32[1,2048]{1,0:T(1,128)} %bitcast.9, f32[1,128]{1,0:T(1,128)} %bitcast.10, s32[1,128]{1,0:T(1,128)} %bitcast.11, s32[1,128]{1,0:T(1,128)} %bitcast.12, s32[1,128]{1,0:T(1,128)} %bitcast.13, bf16[256,1024]{1,0:T(8,128)(2,1)} %res_in.1, ...), custom_call_target="tpu_custom_call" | custom-call | tf_op jit(solution)/shard_map/pallas_call | solution.py:381
  107.2 1.9 %copy.12 = bf16[128,2048]{1,0:T(8,128)(2,1)} copy(bf16[128,2048]{1,0:T(8,128)(2,1)} %shard_map.100) | data formatting | bytes 1048576
